TPU v7x, 32 devices: a whole 2x2x4 slice. The times are simulated.
32 devices in a mesh: group: 2 (over x), rows: 16 (over z, y, core).
Axes of the slice: x: 2, y: 2, z: 4, core: 2. Of those that a mesh axis runs over, the one named last changes fastest.
Arguments:
- basis: bfloat16 [131072, 1024], P(('group', 'rows')), parts along dimension 0
- thermal_load: bfloat16 [32, 131072], P(None, ('group', 'rows')), parts along dimension 1, may hold values from -3 to 3
- pressure_load: bfloat16 [32, 131072], P(None, ('group', 'rows')), parts along dimension 1, may hold values from -3 to 3
- heat_coef: bfloat16 [131072], P(('group', 'rows')), parts along dimension 0, may hold values from 0.5 to 2
- node_pad: int32 [131072], P(('group', 'rows')), parts along dimension 0, may hold values from 0 to 35, as said below
- pad_factor: float32 [72], P('group'), parts along dimension 0, may hold values from 0.3 to 3
- node_owner: int32 [65536, 1], P(('group', 'rows')), parts along dimension 0, may hold values from 0 to 15; in each aligned block of 2048 rows (0 to 2047, 2048 to 4095, ...) at most 256 rows name the same one
- node_row: int32 [65536], P(('group', 'rows')), parts along dimension 0, may hold values from 0 to 4095
- tile_count: int32 [32, 16], P(('group', 'rows')), parts along dimension 0, may hold values from 1 to 128, 1792 in all within a row
- clearance: float32 [65536], P(('group', 'rows')), parts along dimension 0, may hold values from 0.5 to 2
- speed: float32 [32], replicated, may hold values from 0.5 to 2
- mode_scale: float32 [2048], P('group'), parts along dimension 0, may hold values from 0.3 to 3
- modal_flex: bfloat16 [2048, 1024], P('group'), parts along dimension 0, may hold values from -0.1875 to 0.1875
Outputs:
- nodal_deflection: float32 [32, 131072], P(None, ('group', 'rows')), parts along dimension 1
- modal_response: float32 [64, 1024], P('group'), parts along dimension 0
- film_gap: float32 [32, 65536], P(None, ('group', 'rows')), parts along dimension 1
- nodal_press: float32 [32, 131072], P(None, ('group', 'rows')), parts along dimension 1
There are 2 independent parts, one for each index of `group`. A program takes and returns all parts, laid end to end along the dimension named above; an argument that names none is the same for every part. Nothing has to cross between parts.
Inputs may be any that keep to these rules, and one draw needn't show every extreme that they name: `node_owner`: among the 2048 slots of one device, one row block is named at most 256 times, and that bound is reached. `tile_count`: the counts of one device's tiles sum to 1792. `node_pad`: the nodes of each pad form one run of consecutive node indices, the pads in increasing order along the nodes; every pad has nodes.
All inputs are finite; a program needn't handle non-finite values.
Results may differ from a plain program's by a relative error of at most 0.04.
Values sent between devices are 32-bit elements; how exact they have to be, the bound alone decides.
A program may use at most 64 MiB of HBM per device.

v0:
```python
import math

import jax
import jax.numpy as jnp
from jax import lax
from jax.sharding import PartitionSpec as P

LIVE_DEV = 1792


def modal_solve(forcing, mode_scale, modal_flex):
    coupled = jnp.dot(forcing.astype(jnp.bfloat16), modal_flex, preferred_element_type=jnp.float32)
    return mode_scale[None, :] * (forcing + coupled)


def rebuild(response, basis):
    return lax.dot_general(
        response.astype(jnp.bfloat16),
        basis,
        (((1,), (1,)), ((), ())),
        preferred_element_type=jnp.float32,
    )


def on_device(
    basis,
    thermal_load,
    pressure_load,
    heat_coef,
    node_pad,
    pad_factor,
    node_owner,
    node_row,
    tile_count,
    clearance,
    speed,
    mode_scale,
    modal_flex,
):
    blocks = lax.axis_size("rows")
    rows_dev = basis.shape[0]
    node_total = rows_dev * blocks
    proj_scale = math.sqrt(basis.shape[1] / node_total)
    slot_total = node_row.shape[0]
    capacity = 2 * slot_total // blocks
    tile_pts = slot_total // tile_count.shape[1]
    pad_count = pad_factor.shape[0]
    live_all = LIVE_DEV * blocks
    counts_rep = jnp.repeat(tile_count[0], tile_pts, total_repeat_length=slot_total)
    live_slot = jnp.arange(slot_total, dtype=jnp.int32) % tile_pts < counts_rep
    owner_block = node_owner[:, 0]
    onehot = (owner_block[:, None] == jnp.arange(blocks, dtype=jnp.int32)[None, :]).astype(
        jnp.int32
    )
    before = jnp.cumsum(onehot, axis=0) - onehot
    slot_pos = jnp.sum(before * onehot, axis=1)
    slot_place = owner_block * capacity + slot_pos
    request = (
        jnp.full((blocks * capacity,), -1, jnp.int32)
        .at[slot_place]
        .set(jnp.where(live_slot, node_row, -1))
    )
    asked_rows = lax.all_to_all(
        request.reshape(blocks, capacity), "rows", split_axis=0, concat_axis=0, tiled=True
    ).reshape(-1)
    valid_ask = asked_rows >= 0
    safe_rows = jnp.where(valid_ask, asked_rows, 0)

    def fetch_slots(field):
        picked = jnp.where(valid_ask[None, :], field[:, safe_rows], 0.0)
        returned = lax.all_to_all(picked, "rows", split_axis=1, concat_axis=1, tiled=True)
        return jnp.where(live_slot[None, :], returned[:, slot_place], 0.0)

    load_one = (thermal_load.astype(jnp.float32) + pressure_load.astype(jnp.float32)).astype(
        jnp.bfloat16
    )
    modal_one = lax.psum(
        proj_scale * jnp.dot(load_one, basis, preferred_element_type=jnp.float32), "rows"
    )
    resp_one = modal_solve(modal_one, mode_scale, modal_flex)
    field_one = rebuild(resp_one, basis)
    defl_one = fetch_slots(field_one)
    gap_one = clearance[None, :] * jnp.exp(jnp.tanh(0.25 * defl_one))
    film_press = jnp.where(live_slot[None, :], speed[:, None] / (gap_one * gap_one), 0.0)
    outgoing = (
        jnp.zeros((film_press.shape[0], blocks * capacity), jnp.float32)
        .at[:, slot_place]
        .set(film_press)
    )
    incoming = lax.all_to_all(outgoing, "rows", split_axis=1, concat_axis=1, tiled=True)
    nodal_press = (
        jnp.zeros((film_press.shape[0], rows_dev), jnp.float32)
        .at[:, safe_rows]
        .add(jnp.where(valid_ask[None, :], incoming, 0.0))
    )
    pad_ids = jnp.arange(pad_count, dtype=jnp.int32)
    mask_rows = (node_pad[:, None] == pad_ids[None, :]).astype(jnp.float32)
    force_local = jnp.dot(nodal_press, mask_rows, precision=lax.Precision.HIGHEST)
    pad_mask = node_pad[None, :] == pad_ids[:, None]
    weighted = jnp.where(pad_mask, heat_coef[None, :], jnp.zeros((), jnp.bfloat16))
    b_local = proj_scale * jnp.dot(weighted, basis, preferred_element_type=jnp.float32)
    pr_local = proj_scale * jnp.dot(
        nodal_press.astype(jnp.bfloat16), basis, preferred_element_type=jnp.float32
    )
    pad_total = lax.psum(force_local, "rows")
    pad_heat = pad_total * pad_factor[None, :] * (pad_count / live_all)
    second_local = pr_local + jnp.dot(pad_heat, b_local, precision=lax.Precision.HIGHEST)
    modal_two = modal_one + lax.psum(second_local, "rows")
    modal_response = modal_solve(modal_two, mode_scale, modal_flex)
    nodal_deflection = rebuild(modal_response, basis)
    defl_two = fetch_slots(nodal_deflection)
    film_gap = jnp.where(
        live_slot[None, :], clearance[None, :] * jnp.exp(jnp.tanh(0.25 * defl_two)), 0.0
    )
    return (nodal_deflection, modal_response, film_gap, nodal_press)


def solution(mesh):
    return jax.shard_map(
        on_device,
        mesh=mesh,
        in_specs=(
            P(("group", "rows"), None),
            P(None, ("group", "rows")),
            P(None, ("group", "rows")),
            P(("group", "rows")),
            P(("group", "rows")),
            P("group"),
            P(("group", "rows"), None),
            P(("group", "rows")),
            P(("group", "rows"), None),
            P(("group", "rows")),
            P(),
            P("group"),
            P("group", None),
        ),
        out_specs=(
            P(None, ("group", "rows")),
            P("group", None),
            P(None, ("group", "rows")),
            P(None, ("group", "rows")),
        ),
        check_vma=False,
    )
```

profile of v0, /device:TPU:0, one launch (start us, length us, event | category | flops | bytes accessed | tf_op | source)
XLA Modules:
  0.0 476.7 jit_solution(9209543993565850049)
XLA Ops:
  7.2 0.0 copy-start
  7.2 1.9 fusion.44
  9.2 4.5 compare_select_fusion.4
  13.7 0.2 compare_reduce_fusion.8
  13.9 0.7 fusion.21
  14.6 4.5 reduce-window.14
  19.1 0.4 slice_reduce_fusion
  19.6 0.2 reduce-window.15
  19.7 0.1 broadcast_add_fusion
  19.8 0.8 fusion.20
  20.6 0.7 compare_select_fusion.3
  21.3 6.3 %broadcast_select_fusion.2 = (s32[2048]{0:T(1024)S(1)}, pred[2048]{0:T(1024)(128)(4,1)S(1)}) fusion(s32[2048]{0:T(1024)} %param.22, pred[2048]{0:T(1024)(128)(4,1)S(1)} %get-tuple-element.48, pred[2048]{0:T(1024)(128)(4,1)S(1)} %get-tuple-element.47, pred[2048]{0:T(1024)(128)(4,1)S(1)} %get-tuple-element.46, pred[2048]{0:T(1024)(128)(4,1)S(1)} %get-tuple-element.45, ...), kind=kLoop, calls=%fused_computation.92 | loop fusion | flops 53248 | bytes 45092 | tf_op jit(solution)/shard_map/jit(_where)/select_n | solution.py:61
  27.7 8.6 %scatter_custom_fusion = s32[4096]{0:T(1024)} fusion(s32[2048]{0:T(1024)S(1)} %bitcast.103, s32[2048]{0:T(1024)S(1)} %get-tuple-element.49, s32[]{:T(128)} %constant.112.clone.1), kind=kCustom, calls=%fused_computation.88 | custom fusion | bytes 16388 | tf_op jit(solution)/shard_map/scatter | solution.py:61
  36.3 7.4 %all-to-all-start = ((s32[16,1,256]{2,1,0:T(1,128)}), s32[16,1,256]{2,1,0:T(1,128)S(1)}, u32[]{:S(2)}, u32[]{:S(2)}) async-start(s32[16,1,256]{2,1,0:T(1,128)} %bitcast.26), calls=%async_computation | async-start | bytes 32768 | tf_op jit(solution)/shard_map/all_to_all | solution.py:63
  43.7 0.0 copy-start.15
  43.7 0.0 all-reduce.3.cloned.1.call-start
  43.7 5.8 %convolution_multiply_fusion.1 = f32[32,1024]{1,0:T(8,128)} fusion(bf16[4096,1024]{1,0:T(8,128)(2,1)} %param.15, bf16[32,4096]{1,0:T(8,128)(2,1)} %param.17, bf16[32,4096]{1,0:T(8,128)(2,1)} %param.16), kind=kOutput, calls=%fused_computation.11 | convolution fusion | flops 268992512 | bytes 9043968 | tf_op jit(solution)/shard_map/dot_general | solution.py:78
  49.5 0.0 all-reduce.3.cloned.1.call-update
  49.5 0.6 all-to-all-done
  50.2 87.6 %all-reduce.3.cloned.1.call-done = f32[32,1024]{1,0:T(8,128)} async-done(((f32[32,1024]{1,0:T(8,128)}), f32[32,1024]{1,0:T(8,128)}) %all-reduce.3.cloned.1.call-update) | async-done | bytes 131088 | tf_op jit(solution)/shard_map/psum | solution.py:77
  137.9 7.7 %fusion.5 = f32[32,4096]{0,1:T(8,128)} fusion(bf16[4096,1024]{1,0:T(8,128)(2,1)} %param.15, f32[32,1024]{1,0:T(8,128)} %all-reduce.3.cloned.1.call-done, bf16[1024,1024]{1,0:T(8,128)(2,1)S(1)} %copy-done, f32[1024]{0:T(1024)S(1)} %copy-done.15), kind=kOutput, calls=%fused_computation.19 | convolution fusion | flops 335675392 | bytes 11145216 | tf_op jit(solution)/shard_map/dot_general | solution.py:17
  145.6 15.7 %gather_fusion = f32[4096,32]{1,0:T(8,128)} fusion(f32[32,4096]{0,1:T(8,128)} %fusion.5, s32[4096]{0:T(1024)S(1)} %broadcast_clamp_fusion), kind=kCustom, calls=%fused_computation | custom fusion | bytes 1064960 | tf_op jit(solution)/shard_map/gather | solution.py:70
  161.2 2.2 copy.59
  163.4 0.9 broadcast_select_fusion.1
  164.3 6.3 %all-to-all-start.1 = ((f32[32,16,256]{2,0,1:T(8,128)}), f32[32,16,256]{2,0,1:T(8,128)S(1)}, u32[]{:S(2)}, u32[]{:S(2)}) async-start(f32[32,16,256]{2,0,1:T(8,128)} %broadcast_select_fusion.1), calls=%async_computation.1 | async-start | bytes 1048576 | tf_op jit(solution)/shard_map/all_to_all | solution.py:71
  170.6 14.4 %all-to-all-done.1 = f32[32,16,256]{2,0,1:T(8,128)S(1)} async-done(((f32[32,16,256]{2,0,1:T(8,128)}), f32[32,16,256]{2,0,1:T(8,128)S(1)}, u32[]{:S(2)}, u32[]{:S(2)}) %all-to-all-start.1) | async-done | bytes 524320 | tf_op jit(solution)/shard_map/all_to_all | solution.py:71
  185.1 2.0 copy.60
  187.1 7.1 %gather_fusion.1 = f32[2048,32]{1,0:T(8,128)S(1)} fusion(f32[32,4096]{0,1:T(8,128)} %bitcast.93, s32[2048]{0:T(1024)S(1)} %broadcast_clamp_fusion.1), kind=kCustom, calls=%fused_computation.1 | custom fusion | bytes 532480 | tf_op jit(solution)/shard_map/gather | solution.py:72
  194.1 0.3 copy.61
  194.5 0.0 copy-done.11
  194.5 0.1 fusion.15
  194.6 0.3 copy.62
  195.0 7.0 %scatter_custom_fusion.1 = f32[32,4096]{0,1:T(8,128)} fusion(s32[2048]{0:T(1024)S(1)} %bitcast.105, f32[2048,32]{1,0:T(8,128)S(1)} %copy.62, f32[]{:T(128)} %constant.111.clone.1), kind=kCustom, calls=%fused_computation.22 | custom fusion | bytes 524292 | tf_op jit(solution)/shard_map/scatter | solution.py:88
  202.0 3.0 copy.63
  205.0 4.1 all-to-all-start.2
  209.1 0.2 all-reduce.5.cloned.1.call-start
  209.3 4.9 %convolution_multiply_fusion = f32[36,1024]{1,0:T(8,128)S(1)} fusion(bf16[4096,1024]{1,0:T(8,128)(2,1)} %param.15, s32[4096]{0:T(1024)S(1)} %copy-done.5, bf16[4096]{0:T(1024)(128)(2,1)S(1)} %copy-done.8), kind=kOutput, calls=%fused_computation.10 | convolution fusion | flops 302321664 | bytes 8560640 | tf_op jit(solution)/shard_map/dot_general | solution.py:101
  214.3 9.2 %all-to-all-done.2 = f32[32,16,256]{2,0,1:T(8,128)S(1)} async-done(((f32[32,16,256]{2,0,1:T(8,128)}), f32[32,16,256]{2,0,1:T(8,128)S(1)}, u32[]{:S(2)}, u32[]{:S(2)}) %all-to-all-start.2) | async-done | bytes 524320 | tf_op jit(solution)/shard_map/all_to_all | solution.py:90
  223.5 2.0 copy.64
  225.5 4.7 bitcast_select_fusion
  230.2 25.0 %scatter_custom_fusion.2 = f32[32,4096]{0,1:T(8,128)} fusion(s32[4096]{0:T(1024)S(1)} %bitcast.101, f32[32,4096]{0,1:T(8,128)} %bitcast_select_fusion, f32[]{:T(128)} %constant.111.clone.1), kind=kCustom, calls=%fused_computation.7 | custom fusion | flops 131072 | bytes 1048580 | tf_op jit(solution)/shard_map/scatter-add | solution.py:94
  255.3 3.5 fusion.10
  258.8 0.0 copy-start.18
  258.8 0.0 copy-start.16
  258.8 5.1 %convolution_multiply_fusion.2 = f32[32,1024]{1,0:T(8,128)S(1)} fusion(bf16[4096,1024]{1,0:T(8,128)(2,1)} %param.15, f32[32,4096]{0,1:T(8,128)S(1)} %copy-done.1), kind=kOutput, calls=%fused_computation.15 | convolution fusion | flops 268599296 | bytes 9043968 | tf_op jit(solution)/shard_map/dot_general | solution.py:102
  263.9 63.1 %psum.22 = f32[32,36]{1,0:T(8,128)S(1)} all-reduce(f32[32,36]{1,0:T(8,128)S(1)} %fusion.10), channel_id=1, replica_groups=mesh['group'=2,'rows'=16] {'rows'}, use_global_device_ids=true, to_apply=%region_7.8 | all-reduce | flops 1152 | bytes 9216 | tf_op jit(solution)/shard_map/psum | solution.py:105
  326.9 0.9 convolution_add_fusion
  327.8 0.0 all-reduce.5.cloned.1.call-update
  327.9 82.9 %all-reduce.5.cloned.1.call-done = f32[32,1024]{1,0:T(8,128)} async-done(((f32[32,1024]{1,0:T(8,128)}), f32[32,1024]{1,0:T(8,128)}) %all-reduce.5.cloned.1.call-update) | async-done | bytes 131088 | tf_op jit(solution)/shard_map/psum | solution.py:108
  410.8 1.4 fusion.2
  412.2 6.0 %fusion.22 = f32[32,4096]{1,0:T(8,128)S(1)} fusion(bf16[4096,1024]{1,0:T(8,128)(2,1)} %param.15, f32[32,1024]{1,0:T(8,128)S(1)} %fusion.2), kind=kOutput, calls=%fused_computation.48 | convolution fusion | flops 268468224 | bytes 9043968 | tf_op jit(solution)/shard_map/dot_general | solution.py:17
  418.2 0.0 copy-done.4
  418.2 1.9 copy.65
  420.1 15.7 %gather_fusion.2 = f32[4096,32]{1,0:T(8,128)} fusion(f32[32,4096]{0,1:T(8,128)} %copy.65, s32[4096]{0:T(1024)S(1)} %broadcast_clamp_fusion), kind=kCustom, calls=%fused_computation.2 | custom fusion | bytes 1064960 | tf_op jit(solution)/shard_map/gather | solution.py:70
  435.8 2.2 copy.66
  438.0 0.9 broadcast_select_fusion
  438.9 6.3 %all-to-all-start.3 = ((f32[32,16,256]{2,0,1:T(8,128)}), f32[32,16,256]{2,0,1:T(8,128)S(1)}, u32[]{:S(2)}, u32[]{:S(2)}) async-start(f32[32,16,256]{2,0,1:T(8,128)} %broadcast_select_fusion), calls=%async_computation.3 | async-start | bytes 1048576 | tf_op jit(solution)/shard_map/all_to_all | solution.py:71
  445.2 3.0 copy.69
  448.2 11.5 %all-to-all-done.3 = f32[32,16,256]{2,0,1:T(8,128)S(1)} async-done(((f32[32,16,256]{2,0,1:T(8,128)}), f32[32,16,256]{2,0,1:T(8,128)S(1)}, u32[]{:S(2)}, u32[]{:S(2)}) %all-to-all-start.3) | async-done | bytes 524320 | tf_op jit(solution)/shard_map/all_to_all | solution.py:71
  459.7 2.0 copy.67
  461.7 7.1 %gather_fusion.3 = f32[2048,32]{1,0:T(8,128)S(1)} fusion(f32[32,4096]{0,1:T(8,128)} %bitcast.92, s32[2048]{0:T(1024)S(1)} %copy-done.7), kind=kCustom, calls=%fused_computation.3 | custom fusion | bytes 532480 | tf_op jit(solution)/shard_map/gather | solution.py:72
  468.7 0.3 copy.68
  469.0 0.0 copy-done.14
  469.0 0.8 select_bitcast_fusion
  (39 shorter events, 0.1 us)
Async XLA Ops:
  7.2 130.7 %copy-start = (bf16[1024,1024]{1,0:T(8,128)(2,1)S(1)}, bf16[1024,1024]{1,0:T(8,128)(2,1)}, u32[]{:S(2)}) copy-start(bf16[1024,1024]{1,0:T(8,128)(2,1)} %param.27) | copy-start | bytes 6291460
  27.7 166.8 %copy-start.13 = (pred[2048]{0:T(1024)(128)(4,1)}, pred[2048]{0:T(1024)(128)(4,1)S(1)}, u32[]{:S(2)}) copy-start(pred[2048]{0:T(1024)(128)(4,1)S(1)} %get-tuple-element.50) | copy-start | bytes 6148
  36.3 13.9 %all-to-all-start = ((s32[16,1,256]{2,1,0:T(1,128)}), s32[16,1,256]{2,1,0:T(1,128)S(1)}, u32[]{:S(2)}, u32[]{:S(2)}) async-start(s32[16,1,256]{2,1,0:T(1,128)} %bitcast.26), calls=%async_computation | async-start | bytes 32768 | tf_op jit(solution)/shard_map/all_to_all | solution.py:63
  43.7 94.2 %copy-start.15 = (f32[1024]{0:T(1024)S(1)}, f32[1024]{0:T(1024)}, u32[]{:S(2)}) copy-start(f32[1024]{0:T(1024)} %param.26) | copy-start | bytes 12292
  43.7 94.2 %all-reduce.3.cloned.1.call-start = ((), (), s32[]{:S(2)}) async-start(), calls=%async_computation.4 | async-start | bytes 262144 | tf_op jit(solution)/shard_map/psum | solution.py:77
  50.2 113.2 %copy-start.9 = (pred[16,256]{1,0:T(8,128)(4,1)}, pred[16,256]{1,0:T(8,128)(4,1)S(1)}, u32[]{:S(2)}) copy-start(pred[16,256]{1,0:T(8,128)(4,1)S(1)} %fusion.54) | copy-start | bytes 12292
  164.3 20.8 %all-to-all-start.1 = ((f32[32,16,256]{2,0,1:T(8,128)}), f32[32,16,256]{2,0,1:T(8,128)S(1)}, u32[]{:S(2)}, u32[]{:S(2)}) async-start(f32[32,16,256]{2,0,1:T(8,128)} %broadcast_select_fusion.1), calls=%async_computation.1 | async-start | bytes 1048576 | tf_op jit(solution)/shard_map/all_to_all | solution.py:71
  170.6 23.5 %copy-start.6 = (s32[2048]{0:T(1024)}, s32[2048]{0:T(1024)S(1)}, u32[]{:S(2)}) copy-start(s32[2048]{0:T(1024)S(1)} %broadcast_clamp_fusion.1) | copy-start | bytes 24580
  187.0 7.4 %copy-start.11 = (f32[2048]{0:T(1024)S(1)}, f32[2048]{0:T(1024)}, u32[]{:S(2)}) copy-start(f32[2048]{0:T(1024)} %param.24) | copy-start | bytes 24580
  187.0 7.4 %copy-start.17 = (f32[32]{0:T(128)S(1)}, f32[32]{0:T(128)}, u32[]{:S(2)}) copy-start(f32[32]{0:T(128)} %param.25) | copy-start | bytes 388
  202.0 7.3 %copy-start.5 = (s32[4096]{0:T(1024)S(1)}, s32[4096]{0:T(1024)}, u32[]{:S(2)}) copy-start(s32[4096]{0:T(1024)} %param.19) | copy-start | bytes 49156
  202.0 7.3 %copy-start.8 = (bf16[4096]{0:T(1024)(128)(2,1)S(1)}, bf16[4096]{0:T(1024)(128)(2,1)}, u32[]{:S(2)}) copy-start(bf16[4096]{0:T(1024)(128)(2,1)} %param.18) | copy-start | bytes 24580
  205.0 18.6 %all-to-all-start.2 = ((f32[32,16,256]{2,0,1:T(8,128)}), f32[32,16,256]{2,0,1:T(8,128)S(1)}, u32[]{:S(2)}, u32[]{:S(2)}) async-start(f32[32,16,256]{2,0,1:T(8,128)} %copy.63), calls=%async_computation.2 | async-start | bytes 1048576 | tf_op jit(solution)/shard_map/all_to_all | solution.py:90
  209.1 201.7 %all-reduce.5.cloned.1.call-start = ((), (), s32[]{:S(2)}) async-start(), calls=%async_computation.5 | async-start | bytes 262144 | tf_op jit(solution)/shard_map/psum | solution.py:108
  255.3 3.5 copy-start.1
  258.8 68.2 %copy-start.18 = (f32[36]{0:T(128)S(1)}, f32[36]{0:T(128)}, u32[]{:S(2)}) copy-start(f32[36]{0:T(128)} %param.20) | copy-start | bytes 436
  258.8 152.0 %copy-start.3 = (f32[32,1024]{1,0:T(8,128)S(1)}, f32[32,1024]{1,0:T(8,128)}, u32[]{:S(2)}) copy-start(f32[32,1024]{1,0:T(8,128)} %all-reduce.3.cloned.1.call-done) | copy-start | bytes 393220
  258.8 152.0 %copy-start.16 = (f32[1024]{0:T(1024)S(1)}, f32[1024]{0:T(1024)}, u32[]{:S(2)}) copy-start(f32[1024]{0:T(1024)} %param.26) | copy-start | bytes 12292
  412.2 6.0 %copy-start.4 = (f32[32,1024]{1,0:T(8,128)}, f32[32,1024]{1,0:T(8,128)S(1)}, u32[]{:S(2)}) copy-start(f32[32,1024]{1,0:T(8,128)S(1)} %fusion.2) | copy-start | bytes 393220
  418.2 17.6 %copy-start.2 = (f32[32,4096]{1,0:T(8,128)}, f32[32,4096]{1,0:T(8,128)S(1)}, u32[]{:S(2)}) copy-start(f32[32,4096]{1,0:T(8,128)S(1)} %fusion.22) | copy-start | bytes 1572868
  435.8 2.2 copy-start.10
  438.9 20.8 %all-to-all-start.3 = ((f32[32,16,256]{2,0,1:T(8,128)}), f32[32,16,256]{2,0,1:T(8,128)S(1)}, u32[]{:S(2)}, u32[]{:S(2)}) async-start(f32[32,16,256]{2,0,1:T(8,128)} %broadcast_select_fusion), calls=%async_computation.3 | async-start | bytes 1048576 | tf_op jit(solution)/shard_map/all_to_all | solution.py:71
  445.2 16.4 %copy-start.7 = (s32[2048]{0:T(1024)S(1)}, s32[2048]{0:T(1024)}, u32[]{:S(2)}) copy-start(s32[2048]{0:T(1024)} %copy-done.6) | copy-start | bytes 24580
  461.6 7.4 %copy-start.12 = (f32[2048]{0:T(1024)S(1)}, f32[2048]{0:T(1024)}, u32[]{:S(2)}) copy-start(f32[2048]{0:T(1024)} %param.24) | copy-start | bytes 24580
  461.6 7.4 %copy-start.14 = (pred[2048]{0:T(1024)(128)(4,1)S(1)}, pred[2048]{0:T(1024)(128)(4,1)}, u32[]{:S(2)}) copy-start(pred[2048]{0:T(1024)(128)(4,1)} %copy-done.13) | copy-start | bytes 6148
Sparse Core Ops, SparseCore 0:
  49.7 88.1 all-reduce.2
  328.0 82.7 all-reduce.4
where the time goes:
time: 478 us; the launch traced here: 477 us
  waiting for transfers between devices  206 us (43%)
  local copies, waits for them, and re-layouts  82.6 us (17%)
  blocking collectives  63.1 us (13%)
  other arithmetic  50.5 us (11%)
  matrix products  35.3 us (7%)
  starting transfers between devices  24.4 us (5%)
  between operations  14.4 us (3%)
    psum x1, waiting for transfers between devices, on_device(): lax.psum(proj_scale * jnp.dot(load_one, basis, preferred_element_type=jnp...  87.6 us
    psum x1, waiting for transfers between devices, on_device(): modal_two = modal_one + lax.psum(second_local, 'rows')  82.9 us
    psum x1, blocking collectives, on_device(): pad_total = lax.psum(force_local, 'rows')  63.1 us
    gather x4, local copies, waits for them, and re-layouts, fetch_slots(): picked = jnp.where(valid_ask[None, :], field[:, safe_rows], 0.0)  35.7 us
    all_to_all x2, waiting for transfers between devices, fetch_slots(): lax.all_to_all(picked, 'rows', split_axis=1, concat_axis=1, tiled=True)  25.9 us
    scatter-add x1, other arithmetic, on_device(): nodal_press = jnp.zeros((film_press.shape[0], rows_dev), jnp.float32).at[...  25 us
    gather x4, local copies, waits for them, and re-layouts, fetch_slots(): return jnp.where(live_slot[None, :], returned[:, slot_place], 0.0)  14.7 us
    dot_general x2, matrix products, rebuild(): lax.dot_general(response.astype(jnp.bfloat16), basis, (((1,), (1,)), ((),...  13.7 us
  transfers between devices with their start and end apart: 6, of which 6 were waited for; matrix products, arithmetic and copies ran while one was open for 3% of the time, Pallas kernels for 0%

commit v1 on v0

v1 whole, which is shorter than its diff:
```python
import functools
import math

import jax
import jax.numpy as jnp
from jax import lax
from jax.experimental import pallas as pl
from jax.experimental.pallas import tpu as pltpu
from jax.sharding import PartitionSpec as P

LIVE_DEV = 1792
LANES = 128
F32 = jnp.float32
BF16 = jnp.bfloat16
NT = (((1,), (1,)), ((), ()))


def dot(a, b):
    return jnp.dot(a, b, preferred_element_type=F32)


def dot_nt(a, b):
    return lax.dot_general(a, b, NT, preferred_element_type=F32)


def kernel(
    n,
    own,
    basis_h,
    thermal,
    pressure,
    heat_coef,
    node_pad,
    pad_factor,
    owner,
    row,
    live,
    clear,
    speed,
    mode_scale,
    flex_h,
    defl_o,
    resp_o,
    gap_o,
    press_o,
    basis,
    flex,
    xs,
    padm,
    wp,
    rw,
    wl,
    qs,
    rq,
    rank,
    s1,
    r1,
    g1,
    hb,
    rh,
    s2,
    r2,
    g2,
    fs,
    rf,
    acc,
    bsem,
    ssem,
    rsem,
):
    me = lax.axis_index("rows")
    cases, modes = resp_o.shape
    nodes = basis.shape[0]
    slots = row.shape[1]
    pads_r = rh.shape[1]
    piece = s1.shape[1]
    capp = rq.shape[2]
    his = nodes // LANES
    chunks = bsem.shape[0] - 1
    rows_c = nodes // chunks
    proj_scale = math.sqrt(modes / (nodes * n))
    per_row = cases // piece

    for i in range(chunks):
        part = pl.ds(i * rows_c, rows_c)
        pltpu.make_async_copy(basis_h.at[part], basis.at[part], bsem.at[i]).start()
    flex_copy = pltpu.make_async_copy(flex_h, flex, bsem.at[chunks])
    flex_copy.start()

    barrier = pltpu.get_barrier_semaphore()

    def greet(k, c):
        pl.semaphore_signal(barrier, inc=1, device_id={"rows": lax.rem(me + k, n)})
        return c

    lax.fori_loop(1, n, greet, 0)

    def remote(phase, k, src, dst, peer):
        return pltpu.make_async_remote_copy(
            src_ref=src,
            dst_ref=dst,
            send_sem=ssem.at[phase, k],
            recv_sem=rsem.at[phase, k],
            device_id={"rows": peer},
        )

    def each(body):
        def step(k, c):
            body(k, lax.rem(me + k, n), lax.rem(me + n - k, n))
            return c

        lax.fori_loop(1, n, step, 0)

    def only(cond, body):
        if own == n:
            body()
        else:
            pl.when(cond)(body)

    ids = owner[...]
    rows = row[...]
    row_hi = lax.shift_right_logical(rows, 7)
    row_lo = rows & (LANES - 1)
    step_c = 256
    strict = (
        lax.broadcasted_iota(jnp.int32, (step_c, step_c), 0)
        < lax.broadcasted_iota(jnp.int32, (step_c, step_c), 1)
    ).astype(BF16)
    oh_o = (lax.broadcasted_iota(jnp.int32, (n, slots), 0) == ids).astype(F32)
    carry = jnp.zeros((n, 1), F32)
    for b in range(slots // step_c):
        part = oh_o[:, b * step_c : (b + 1) * step_c]
        before = dot(part.astype(BF16), strict) + carry
        carry = carry + jnp.sum(part, axis=1, keepdims=True)
        rank[:, b * step_c : (b + 1) * step_c] = jnp.sum(
            part * before, axis=0, keepdims=True
        ).astype(jnp.int32)
    oh_p = (lax.broadcasted_iota(jnp.int32, (capp, slots), 0) == rank[...]).astype(F32).astype(BF16)
    asked = dot_nt((oh_o * row_hi.astype(F32)).astype(BF16), oh_p) * float(LANES) + dot_nt(
        (oh_o * row_lo.astype(F32)).astype(BF16), oh_p
    )
    asked = asked.astype(jnp.int32)
    for o in range(n):
        qs[o] = asked[o : o + 1, :]

    inv = 1.0 / clear[...]
    weight = live[...] * inv * inv
    w_hi = weight.astype(BF16).astype(F32)
    w_lo = weight - w_hi
    lo_hit = lax.broadcasted_iota(jnp.int32, (LANES, slots), 0) == row_lo
    b_w = jnp.concatenate(
        [jnp.where(lo_hit, w_hi, 0.0).astype(BF16), jnp.where(lo_hit, w_lo, 0.0).astype(BF16)], axis=0
    )
    node_hi = ids * his + row_hi
    for o in range(0, n, 16):
        rows_o = 16 * his
        a_w = (
            (lax.broadcasted_iota(jnp.int32, (rows_o, slots), 0) + o * his == node_hi)
            .astype(F32)
            .astype(BF16)
        )
        both = dot_nt(a_w, b_w)
        wp[o : o + 16] = (both[:, :LANES] + both[:, LANES:]).reshape(16, his, LANES)

    xs[0:cases, :] = (thermal[...].astype(F32) + pressure[...].astype(F32)).astype(BF16)
    pad_ids = lax.broadcasted_iota(jnp.int32, (padm.shape[0], nodes), 0)
    hit = pad_ids == node_pad[...]
    padm[...] = hit.astype(F32).astype(BF16)
    xs[cases:, :] = jnp.where(
        hit[: xs.shape[0] - cases], heat_coef[...].astype(F32), 0.0
    ).astype(BF16)
    for i in range(chunks):
        part = pl.ds(i * rows_c, rows_c)
        pltpu.make_async_copy(basis_h.at[part], basis.at[part], bsem.at[i]).wait()
        got = dot(xs[:, i * rows_c : (i + 1) * rows_c], basis[part, :])
        if i == 0:
            acc[...] = got
        else:
            acc[...] += got
    for j in range(own):
        blk, r0 = j // per_row, (j % per_row) * piece
        s1[j] = proj_scale * acc[r0 : r0 + piece, blk * LANES : (blk + 1) * LANES]
    for m in range(modes // LANES):
        hb[m] = proj_scale * acc[cases : cases + pads_r, m * LANES : (m + 1) * LANES]

    pl.semaphore_wait(barrier, n - 1)

    def first_copy(k, peer):
        return remote(0, k, s1.at[peer], r1.at[k], peer)

    each(lambda k, to, fr: only(to < own, lambda: first_copy(k, to).start()))

    def weight_copy(k, peer):
        return remote(1, k, wp.at[peer], rw.at[k], peer)

    def ask_copy(k, peer):
        return remote(2, k, qs.at[peer], rq.at[k], peer)

    def heat_copy(k, peer):
        return remote(3, k, hb.at[lax.div(peer, per_row)], rh.at[k], peer)

    rq[0] = qs[me]

    def reduce_first():
        each(lambda k, to, fr: first_copy(k, to).wait_recv())
        g1[me] = s1[me] + functools.reduce(lambda a, b: a + b, [r1[k] for k in range(1, n)])

    only(me < own, reduce_first)

    def share_copy(phase, g, k, peer):
        return remote(phase, k, g.at[me], g.at[me], peer)

    def share_wait(phase, g, k, fr):
        remote(phase, k, g.at[fr], g.at[fr], fr).wait_recv()

    only(me < own, lambda: each(lambda k, to, fr: share_copy(4, g1, k, to).start()))
    each(lambda k, to, fr: weight_copy(k, to).start())
    each(lambda k, to, fr: ask_copy(k, to).start())
    each(lambda k, to, fr: only(to < own, lambda: heat_copy(k, to).start()))
    each(lambda k, to, fr: only(fr < own, lambda: share_wait(4, g1, k, fr)))

    def gathered(g):
        flat = g[...].reshape(own * piece, LANES)
        return jnp.concatenate(
            [flat[m * cases : (m + 1) * cases] for m in range(modes // LANES)], axis=1
        )

    def solve(forcing):
        return mode_scale[...] * (forcing + dot(forcing.astype(BF16), flex[...]))

    flex_copy.wait()
    resp = solve(gathered(g1)).astype(BF16)

    each(lambda k, to, fr: weight_copy(k, to).wait_recv())
    wl[...] = wp[me] + functools.reduce(lambda a, b: a + b, [rw[k] for k in range(1, n)])
    pad_part = jnp.zeros((cases, padm.shape[0]), F32)
    for i in range(chunks):
        lo, hi = i * rows_c, (i + 1) * rows_c
        field = dot_nt(resp, basis[lo:hi, :])
        w_row = jnp.concatenate(
            [wl[h : h + 1, :] for h in range(lo // LANES, hi // LANES)], axis=1
        )
        press = speed[...] * jnp.exp(-2.0 * jnp.tanh(0.25 * field)) * w_row
        press_o[:, lo:hi] = press
        press = press.astype(BF16)
        got = dot(press, basis[lo:hi, :])
        if i == 0:
            acc[0:cases, :] = got
        else:
            acc[0:cases, :] += got
        pad_part = pad_part + dot_nt(press, padm[:, lo:hi])
    for j in range(own):
        blk, r0 = j // per_row, (j % per_row) * piece
        s2[j, 0:piece] = proj_scale * acc[r0 : r0 + piece, blk * LANES : (blk + 1) * LANES]
        s2[j, piece:] = pad_part[r0 : r0 + piece, :]

    def second_copy(k, peer):
        return remote(5, k, s2.at[peer], r2.at[k], peer)

    each(lambda k, to, fr: only(to < own, lambda: second_copy(k, to).start()))

    def reduce_second():
        each(lambda k, to, fr: heat_copy(k, to).wait_recv())
        heat = hb[lax.div(me, per_row)] + functools.reduce(
            lambda a, b: a + b, [rh[k] for k in range(1, n)]
        )
        heat = jnp.concatenate([heat, jnp.zeros((LANES - pads_r, LANES), F32)], axis=0)
        each(lambda k, to, fr: second_copy(k, to).wait_recv())
        total = s2[me] + functools.reduce(lambda a, b: a + b, [r2[k] for k in range(1, n)])
        pad_heat = total[piece:] * pad_factor[...]
        g2[me] = (
            g1[me]
            + total[:piece]
            + jnp.dot(pad_heat, heat, precision=lax.Precision.HIGHEST, preferred_element_type=F32)
        )

    only(me < own, reduce_second)
    only(me < own, lambda: each(lambda k, to, fr: share_copy(6, g2, k, to).start()))
    each(lambda k, to, fr: only(fr < own, lambda: share_wait(6, g2, k, fr)))
    resp2 = solve(gathered(g2))
    resp_o[...] = resp2
    resp2 = resp2.astype(BF16)
    for i in range(chunks):
        lo, hi = i * rows_c, (i + 1) * rows_c
        defl_o[:, lo:hi] = dot_nt(resp2, basis[lo:hi, :])

    each(lambda k, to, fr: ask_copy(k, to).wait_recv())

    def pick(k):
        out = []
        for c in range(capp // LANES):
            idx = jnp.broadcast_to(rq[k][:, c * LANES : (c + 1) * LANES], (cases, LANES))
            idx_hi = lax.shift_right_logical(idx, 7)
            idx_lo = idx & (LANES - 1)
            val = jnp.zeros((cases, LANES), F32)
            for h in range(his):
                got = jnp.take_along_axis(defl_o[:, h * LANES : (h + 1) * LANES], idx_lo, axis=1)
                val = jnp.where(idx_hi == h, got, val)
            out.append(val)
        return jnp.concatenate(out, axis=1) if len(out) > 1 else out[0]

    def answer_copy(k, peer):
        return remote(7, k, fs.at[k], rf.at[me], peer)

    def answer(k, to, fr):
        fs[k] = pick(k)
        answer_copy(k, fr).start()

    each(answer)
    rf[me] = pick(0)
    each(lambda k, to, fr: remote(7, k, fs.at[k], rf.at[to], to).wait_recv())

    def place(t, c):
        part = pl.ds(pl.multiple_of(t * LANES, LANES), LANES)
        own_t = jnp.broadcast_to(owner[:, part], (cases, LANES))
        pos_t = jnp.broadcast_to(rank[:, part], (cases, LANES))
        blk = own_t * (capp // LANES) + lax.shift_right_logical(pos_t, 7)
        lane = pos_t & (LANES - 1)
        val = jnp.zeros((cases, LANES), F32)
        for o in range(n):
            for s in range(capp // LANES):
                got = jnp.take_along_axis(rf[o, :, s * LANES : (s + 1) * LANES], lane, axis=1)
                val = jnp.where(blk == o * (capp // LANES) + s, got, val)
        gap_o[:, part] = live[:, part] * clear[:, part] * jnp.exp(jnp.tanh(0.25 * val))
        return c

    lax.fori_loop(0, slots // LANES, place, 0)

    def drain(k, to, fr):
        def owned():
            first_copy(k, to).wait_send()
            heat_copy(k, to).wait_send()
            second_copy(k, to).wait_send()

        def mine():
            share_copy(4, g1, k, to).wait_send()
            share_copy(6, g2, k, to).wait_send()

        weight_copy(k, to).wait_send()
        ask_copy(k, to).wait_send()
        answer_copy(k, fr).wait_send()
        only(to < own, owned)
        only(me < own, mine)

    each(drain)


def on_device(
    basis,
    thermal_load,
    pressure_load,
    heat_coef,
    node_pad,
    pad_factor,
    node_owner,
    node_row,
    tile_count,
    clearance,
    speed,
    mode_scale,
    modal_flex,
):
    n = lax.axis_size("rows")
    nodes, modes = basis.shape
    cases = thermal_load.shape[0]
    slots = node_row.shape[0]
    capacity = 2 * slots // n
    capp = max(LANES, -(-capacity // LANES) * LANES)
    tiles = tile_count.shape[1]
    tile_pts = slots // tiles
    pads = pad_factor.shape[0]
    pads_r = -(-pads // 8) * 8
    pads_x = -(-pads // 16) * 16
    all_tiles = cases * modes // LANES
    own = min(n, all_tiles // 8)
    piece = all_tiles // own
    his = nodes // LANES
    chunks = 8

    live = (
        (jnp.arange(tile_pts, dtype=jnp.int32)[None, :] < tile_count[0][:, None])
        .astype(F32)
        .reshape(1, slots)
    )
    factor = jnp.zeros((1, LANES), F32).at[0, :pads].set(pad_factor * (pads / (LIVE_DEV * n)))

    vmem = pl.BlockSpec(memory_space=pltpu.VMEM)
    anyw = pl.BlockSpec(memory_space=pl.ANY)
    return pl.pallas_call(
        functools.partial(kernel, n, own),
        out_shape=(
            jax.ShapeDtypeStruct((cases, nodes), F32),
            jax.ShapeDtypeStruct((cases, modes), F32),
            jax.ShapeDtypeStruct((cases, slots), F32),
            jax.ShapeDtypeStruct((cases, nodes), F32),
        ),
        in_specs=[anyw] + [vmem] * 11 + [anyw],
        out_specs=(vmem,) * 4,
        scratch_shapes=[
            pltpu.VMEM((nodes, modes), BF16),
            pltpu.VMEM((modes, modes), BF16),
            pltpu.VMEM((cases + pads_x, nodes), BF16),
            pltpu.VMEM((LANES, nodes), BF16),
            pltpu.VMEM((n, his, LANES), F32),
            pltpu.VMEM((n, his, LANES), F32),
            pltpu.VMEM((his, LANES), F32),
            pltpu.VMEM((n, 1, capp), jnp.int32),
            pltpu.VMEM((n, 1, capp), jnp.int32),
            pltpu.VMEM((1, slots), jnp.int32),
            pltpu.VMEM((own, piece, LANES), F32),
            pltpu.VMEM((n, piece, LANES), F32),
            pltpu.VMEM((own, piece, LANES), F32),
            pltpu.VMEM((modes // LANES, pads_r, LANES), F32),
            pltpu.VMEM((n, pads_r, LANES), F32),
            pltpu.VMEM((own, 2 * piece, LANES), F32),
            pltpu.VMEM((n, 2 * piece, LANES), F32),
            pltpu.VMEM((own, piece, LANES), F32),
            pltpu.VMEM((n, cases, capp), F32),
            pltpu.VMEM((n, cases, capp), F32),
            pltpu.VMEM((cases + pads_x, modes), F32),
            pltpu.SemaphoreType.DMA((chunks + 1,)),
            pltpu.SemaphoreType.DMA((8, n)),
            pltpu.SemaphoreType.DMA((8, n)),
        ],
        compiler_params=pltpu.CompilerParams(
            collective_id=0, has_side_effects=True, vmem_limit_bytes=56 * 1024 * 1024
        ),
    )(
        basis,
        thermal_load,
        pressure_load,
        heat_coef.reshape(1, nodes),
        node_pad.reshape(1, nodes),
        factor,
        node_owner.reshape(1, slots),
        node_row.reshape(1, slots),
        live,
        clearance.reshape(1, slots),
        speed.reshape(cases, 1),
        mode_scale.reshape(1, modes),
        modal_flex,
    )


def solution(mesh):
    return jax.shard_map(
        on_device,
        mesh=mesh,
        in_specs=(
            P(("group", "rows"), None),
            P(None, ("group", "rows")),
            P(None, ("group", "rows")),
            P(("group", "rows")),
            P(("group", "rows")),
            P("group"),
            P(("group", "rows"), None),
            P(("group", "rows")),
            P(("group", "rows"), None),
            P(("group", "rows")),
            P(),
            P("group"),
            P("group", None),
        ),
        out_specs=(
            P(None, ("group", "rows")),
            P("group", None),
            P(None, ("group", "rows")),
            P(None, ("group", "rows")),
        ),
        check_vma=False,
    )
```

time: 478 us -> 87.1 us (0.18)
  waiting for transfers between devices: 206 us -> 0 us
  Pallas kernels: 0 us -> 72.7 us
  local copies, waits for them, and re-layouts: 82.6 us -> 10.1 us
  blocking collectives: 63.1 us -> 0 us
  other arithmetic: 50.5 us -> 3.27 us
  matrix products: 35.3 us -> 0 us
  starting transfers between devices: 24.4 us -> 0 us
  between operations: 14.4 us -> 0.64 us
    psum x2 -> x0, waiting for transfers between devices: 171 us -> none  [the longest x1 87.6 us: on_device(): lax.psum(proj_scale * jnp.dot(load_one, basis, preferred_element_type=jnp...]
    pallas_call x0 -> x1, Pallas kernels: none -> 72.7 us  [on_device(): pl.pallas_call(functools.partial(kernel, n, own), out_shape=(jax.ShapeDty...]
    psum x1 -> x0, blocking collectives: 63.1 us -> none  [on_device(): pad_total = lax.psum(force_local, 'rows')]
    gather x9 -> x0, local copies, waits for them, and re-layouts: 52.4 us -> none  [the longest x4 35.7 us: fetch_slots(): picked = jnp.where(valid_ask[None, :], field[:, safe_rows], 0.0)]
    all_to_all x4 -> x0, waiting for transfers between devices: 35.8 us -> none  [the longest x2 25.9 us: fetch_slots(): lax.all_to_all(picked, 'rows', split_axis=1, concat_axis=1, tiled=True)]
    dot_general x8 -> x0, matrix products: 35.3 us -> none  [the longest x2 13.7 us: rebuild(): lax.dot_general(response.astype(jnp.bfloat16), basis, (((1,), (1,)), ((),...]
    scatter-add x1 -> x0, other arithmetic: 25 us -> none  [on_device(): nodal_press = jnp.zeros((film_press.shape[0], rows_dev), jnp.float32).at[...]
    all_to_all x4 -> x0, starting transfers between devices: 24.2 us -> none  [the longest x2 12.7 us: fetch_slots(): lax.all_to_all(picked, 'rows', split_axis=1, concat_axis=1, tiled=True)]
  transfers between devices with their start and end apart: 6 -> 0, of which waited for: 6 -> 0; matrix products, arithmetic and copies ran while one was open for 3% -> 0% of each run, Pallas kernels for 0% -> 0%
where the time goes in v1:
time: 87.1 us; the launch traced here: 86.7 us
  Pallas kernels  72.7 us (83%)
  local copies, waits for them, and re-layouts  10.1 us (12%)
  other arithmetic  3.27 us (4%)
    pallas_call x1, Pallas kernels, on_device(): pl.pallas_call(functools.partial(kernel, n, own), out_shape=(jax.ShapeDty...  72.7 us
    unnamed x4, local copies, waits for them, and re-layouts  6.97 us
    another operation x2, other arithmetic  1.94 us

profile of v1, /device:TPU:0, one launch (start us, length us, event | category | flops | bytes accessed | tf_op | source)
XLA Modules:
  0.0 86.7 jit_solution(397081794860370951)
XLA Ops:
  0.6 0.6 compare_reduce_fusion
  1.3 1.3 %fusion.1 = f32[1,36]{1,0:T(1,128)S(1)} fusion(pred[]{:T(512)} %compare_reduce_fusion, f32[36]{0:T(128)} %param.20), kind=kLoop, calls=%fused_computation.4 | loop fusion | flops 72 | bytes 289 | tf_op jit(solution)/shard_map/reshape.39
  2.6 0.5 scatter.4.pad_factor
  3.1 1.3 %fusion = f32[16,128]{1,0:T(8,128)} fusion(s32[16]{0:T(128)} %bitcast.16), kind=kLoop, calls=%fused_computation.1 | loop fusion | flops 4096 | bytes 8256 | tf_op jit(solution)/shard_map/convert_element_type | solution.py:382
  4.4 1.3 %reshape.88.heat_coef = bf16[1,4096]{1,0:T(2,128)(2,1)} reshape(bf16[4096]{0:T(1024)(128)(2,1)} %param.18) | data formatting | bytes 16384 | tf_op jit(solution)/shard_map/reshape | solution.py:432
  5.7 1.3 %copy.17.speed = f32[32,1]{1,0:T(8,128)} copy(f32[32,1]{0,1:T(1,128)} %bitcast.17) | data formatting | bytes 256 | tf_op jit(solution)/shard_map/reshape | solution.py:439
  7.1 72.7 %shard_map.156 = (f32[32,4096]{1,0:T(8,128)}, f32[32,1024]{1,0:T(8,128)}, f32[32,2048]{1,0:T(8,128)}, f32[32,4096]{1,0:T(8,128)}) custom-call(bf16[4096,1024]{1,0:T(8,128)(2,1)} %basis_h.1, bf16[32,4096]{1,0:T(8,128)(2,1)} %thermal.1, bf16[32,4096]{1,0:T(8,128)(2,1)} %pressure.1, bf16[1,4096]{1,0:T(2,128)(2,1)} %reshape.88.heat_coef, s32[1,4096]{1,0:T(1,128)} %bitcast.11, ...), custom_call_target="tpu_custom_call" | custom-call | tf_op jit(solution)/shard_map/pallas_call | solution.py:389
  79.8 1.9 %copy.22 = f32[32,4096]{1,0:T(8,128)} copy(f32[32,4096]{1,0:T(8,128)} %get-tuple-element.20) | data formatting | bytes 1048576
  81.6 1.6 %copy.23 = f32[32,1024]{1,0:T(8,128)} copy(f32[32,1024]{1,0:T(8,128)} %get-tuple-element.21) | data formatting | bytes 262144
  83.2 1.7 %copy.24 = f32[32,2048]{1,0:T(8,128)} copy(f32[32,2048]{1,0:T(8,128)} %get-tuple-element.22) | data formatting | bytes 524288
  84.9 1.9 %copy.25 = f32[32,4096]{1,0:T(8,128)} copy(f32[32,4096]{1,0:T(8,128)} %get-tuple-element.23) | data formatting | bytes 1048576

commit v2 on v1

--- a/solution.py
+++ b/solution.py
@@ -34,11 +34,15 @@
     pad_factor,
     owner,
     row,
-    live,
+    tile_count,
     clear,
     speed,
     mode_scale,
     flex_h,
+    defl_h,
+    resp_h,
+    gap_h,
+    press_h,
     defl_o,
     resp_o,
     gap_o,
@@ -47,8 +51,7 @@
     flex,
     xs,
     padm,
-    wp,
-    rw,
+    live,
     wl,
     qs,
     rq,
@@ -58,6 +61,7 @@
     g1,
     hb,
     rh,
+    hfull,
     s2,
     r2,
     g2,
@@ -65,6 +69,7 @@
     rf,
     acc,
     bsem,
+    osem,
     ssem,
     rsem,
 ):
@@ -72,7 +77,8 @@
     cases, modes = resp_o.shape
     nodes = basis.shape[0]
     slots = row.shape[1]
-    pads_r = rh.shape[1]
+    rows_h = rh.shape[1]
+    pads_r = xs.shape[0] - cases
     piece = s1.shape[1]
     capp = rq.shape[2]
     his = nodes // LANES
@@ -80,6 +86,8 @@
     rows_c = nodes // chunks
     proj_scale = math.sqrt(modes / (nodes * n))
     per_row = cases // piece
+    packed = s2.shape[1] - piece < piece
+    half = LANES // 2
 
     for i in range(chunks):
         part = pl.ds(i * rows_c, rows_c)
@@ -105,7 +113,8 @@
         )
 
     def each(body):
-        def step(k, c):
+        def step(i, c):
+            k = n // 2 + lax.div(i, 2) * (1 - 2 * lax.rem(i, 2))
             body(k, lax.rem(me + k, n), lax.rem(me + n - k, n))
             return c
 
@@ -136,39 +145,38 @@
             part * before, axis=0, keepdims=True
         ).astype(jnp.int32)
     oh_p = (lax.broadcasted_iota(jnp.int32, (capp, slots), 0) == rank[...]).astype(F32).astype(BF16)
-    asked = dot_nt((oh_o * row_hi.astype(F32)).astype(BF16), oh_p) * float(LANES) + dot_nt(
-        (oh_o * row_lo.astype(F32)).astype(BF16), oh_p
-    )
-    asked = asked.astype(jnp.int32)
-    for o in range(n):
-        qs[o] = asked[o : o + 1, :]
-
+    tiles = tile_count.shape[1]
+    lane_id = lax.broadcasted_iota(jnp.int32, (1, slots), 1)
+    spread = lax.div(lax.broadcasted_iota(jnp.int32, (tiles, slots), 1), slots // tiles)
+    spread = (spread == lax.broadcasted_iota(jnp.int32, (tiles, slots), 0)).astype(F32).astype(BF16)
+    counts = jnp.broadcast_to(tile_count[...].astype(F32), (8, tiles)).astype(BF16)
+    counts = dot(counts, spread)[0:1, :]
+    live[...] = (lax.rem(lane_id, slots // tiles).astype(F32) < counts).astype(F32)
     inv = 1.0 / clear[...]
     weight = live[...] * inv * inv
     w_hi = weight.astype(BF16).astype(F32)
-    w_lo = weight - w_hi
-    lo_hit = lax.broadcasted_iota(jnp.int32, (LANES, slots), 0) == row_lo
-    b_w = jnp.concatenate(
-        [jnp.where(lo_hit, w_hi, 0.0).astype(BF16), jnp.where(lo_hit, w_lo, 0.0).astype(BF16)], axis=0
-    )
-    node_hi = ids * his + row_hi
-    for o in range(0, n, 16):
-        rows_o = 16 * his
-        a_w = (
-            (lax.broadcasted_iota(jnp.int32, (rows_o, slots), 0) + o * his == node_hi)
-            .astype(F32)
-            .astype(BF16)
-        )
-        both = dot_nt(a_w, b_w)
-        wp[o : o + 16] = (both[:, :LANES] + both[:, LANES:]).reshape(16, his, LANES)
+    parts = (row_hi.astype(F32), row_lo.astype(F32), w_hi, weight - w_hi)
+    asked = dot_nt(jnp.concatenate([(oh_o * v).astype(BF16) for v in parts], axis=0), oh_p)
+    asked_row = asked[0:n] * float(LANES) + asked[n : 2 * n]
+    asked_w = asked[2 * n : 3 * n] + asked[3 * n :]
+    for o in range(n):
+        qs[o, 0:1] = asked_row[o : o + 1, :]
+        qs[o, 1:2] = asked_w[o : o + 1, :]
+
+    def ask_copy(k, peer):
+        return remote(2, k, qs.at[peer], rq.at[k], peer)
+
+    pl.semaphore_wait(barrier, n - 1)
+    each(lambda k, to, fr: ask_copy(k, to).start())
+    rq[0] = qs[me]
 
     xs[0:cases, :] = (thermal[...].astype(F32) + pressure[...].astype(F32)).astype(BF16)
     pad_ids = lax.broadcasted_iota(jnp.int32, (padm.shape[0], nodes), 0)
-    hit = pad_ids == node_pad[...]
+    hit = (pad_ids & (half - 1)) == node_pad[...]
+    coef = heat_coef[...].astype(F32)
+    coef = jnp.concatenate([coef[h : h + 1, :] for h in range(his)], axis=1)
     padm[...] = hit.astype(F32).astype(BF16)
-    xs[cases:, :] = jnp.where(
-        hit[: xs.shape[0] - cases], heat_coef[...].astype(F32), 0.0
-    ).astype(BF16)
+    xs[cases:, :] = jnp.where(hit[:pads_r], coef, 0.0).astype(BF16)
     for i in range(chunks):
         part = pl.ds(i * rows_c, rows_c)
         pltpu.make_async_copy(basis_h.at[part], basis.at[part], bsem.at[i]).wait()
@@ -180,26 +188,16 @@
     for j in range(own):
         blk, r0 = j // per_row, (j % per_row) * piece
         s1[j] = proj_scale * acc[r0 : r0 + piece, blk * LANES : (blk + 1) * LANES]
-    for m in range(modes // LANES):
-        hb[m] = proj_scale * acc[cases : cases + pads_r, m * LANES : (m + 1) * LANES]
-
-    pl.semaphore_wait(barrier, n - 1)
+        h0 = cases + (j % per_row) * rows_h
+        hb[j] = proj_scale * acc[h0 : h0 + rows_h, blk * LANES : (blk + 1) * LANES]
 
     def first_copy(k, peer):
         return remote(0, k, s1.at[peer], r1.at[k], peer)
 
     each(lambda k, to, fr: only(to < own, lambda: first_copy(k, to).start()))
 
-    def weight_copy(k, peer):
-        return remote(1, k, wp.at[peer], rw.at[k], peer)
-
-    def ask_copy(k, peer):
-        return remote(2, k, qs.at[peer], rq.at[k], peer)
-
     def heat_copy(k, peer):
-        return remote(3, k, hb.at[lax.div(peer, per_row)], rh.at[k], peer)
-
-    rq[0] = qs[me]
+        return remote(3, k, hb.at[peer], rh.at[k], peer)
 
     def reduce_first():
         each(lambda k, to, fr: first_copy(k, to).wait_recv())
@@ -214,9 +212,24 @@
         remote(phase, k, g.at[fr], g.at[fr], fr).wait_recv()
 
     only(me < own, lambda: each(lambda k, to, fr: share_copy(4, g1, k, to).start()))
-    each(lambda k, to, fr: weight_copy(k, to).start())
-    each(lambda k, to, fr: ask_copy(k, to).start())
     each(lambda k, to, fr: only(to < own, lambda: heat_copy(k, to).start()))
+    each(lambda k, to, fr: ask_copy(k, to).wait_recv())
+    both = jnp.zeros((his, 2 * LANES), F32)
+    for k in range(n):
+        idx = rq[k, 0:1].astype(jnp.int32)
+        wgt = rq[k, 1:2]
+        top = wgt.astype(BF16).astype(F32)
+        hi_hit = lax.broadcasted_iota(jnp.int32, (his, capp), 0) == lax.shift_right_logical(idx, 7)
+        lo_hit = lax.broadcasted_iota(jnp.int32, (LANES, capp), 0) == (idx & (LANES - 1))
+        b_w = jnp.concatenate(
+            [jnp.where(lo_hit, top, 0.0), jnp.where(lo_hit, wgt - top, 0.0)], axis=0
+        ).astype(BF16)
+        both = both + dot_nt(hi_hit.astype(F32).astype(BF16), b_w)
+    wl[...] = both[:, :LANES] + both[:, LANES:]
+    eye = lax.broadcasted_iota(jnp.int32, (cases, cases), 0) == lax.broadcasted_iota(
+        jnp.int32, (cases, cases), 1
+    )
+    speed_c = jnp.sum(jnp.where(eye, speed[...], 0.0), axis=1, keepdims=True)
     each(lambda k, to, fr: only(fr < own, lambda: share_wait(4, g1, k, fr)))
 
     def gathered(g):
@@ -231,8 +244,6 @@
     flex_copy.wait()
     resp = solve(gathered(g1)).astype(BF16)
 
-    each(lambda k, to, fr: weight_copy(k, to).wait_recv())
-    wl[...] = wp[me] + functools.reduce(lambda a, b: a + b, [rw[k] for k in range(1, n)])
     pad_part = jnp.zeros((cases, padm.shape[0]), F32)
     for i in range(chunks):
         lo, hi = i * rows_c, (i + 1) * rows_c
@@ -240,7 +251,7 @@
         w_row = jnp.concatenate(
             [wl[h : h + 1, :] for h in range(lo // LANES, hi // LANES)], axis=1
         )
-        press = speed[...] * jnp.exp(-2.0 * jnp.tanh(0.25 * field)) * w_row
+        press = speed_c * jnp.exp(-2.0 * jnp.tanh(0.25 * field)) * w_row
         press_o[:, lo:hi] = press
         press = press.astype(BF16)
         got = dot(press, basis[lo:hi, :])
@@ -249,29 +260,75 @@
         else:
             acc[0:cases, :] += got
         pad_part = pad_part + dot_nt(press, padm[:, lo:hi])
+    low = lax.broadcasted_iota(jnp.int32, (cases, LANES), 1) < half
     for j in range(own):
         blk, r0 = j // per_row, (j % per_row) * piece
         s2[j, 0:piece] = proj_scale * acc[r0 : r0 + piece, blk * LANES : (blk + 1) * LANES]
-        s2[j, piece:] = pad_part[r0 : r0 + piece, :]
+        if packed:
+            mid = r0 + piece // 2
+            s2[j, piece:] = jnp.where(low[r0:mid], pad_part[r0:mid], pad_part[mid : r0 + piece])
+        else:
+            s2[j, piece:] = pad_part[r0 : r0 + piece, :]
+
+    def out_copy(i, src, dst):
+        return pltpu.make_async_copy(src, dst, osem.at[i])
 
     def second_copy(k, peer):
         return remote(5, k, s2.at[peer], r2.at[k], peer)
 
     each(lambda k, to, fr: only(to < own, lambda: second_copy(k, to).start()))
 
+    out_copy(0, press_o, press_h).start()
+    mine_h = lax.rem(me, per_row)
+
+    def mate_copy(d):
+        mate = me - mine_h + lax.rem(mine_h + d, per_row)
+        return pltpu.make_async_remote_copy(
+            src_ref=hfull.at[mine_h],
+            dst_ref=hfull.at[mine_h],
+            send_sem=ssem.at[1, d],
+            recv_sem=rsem.at[1, d],
+            device_id={"rows": mate},
+        )
+
+    def mate_wait(d):
+        other = lax.rem(mine_h + per_row - d, per_row)
+        pltpu.make_async_remote_copy(
+            src_ref=hfull.at[other],
+            dst_ref=hfull.at[other],
+            send_sem=ssem.at[1, d],
+            recv_sem=rsem.at[1, d],
+            device_id={"rows": me - mine_h + other},
+        ).wait_recv()
+
     def reduce_second():
         each(lambda k, to, fr: heat_copy(k, to).wait_recv())
-        heat = hb[lax.div(me, per_row)] + functools.reduce(
+        hfull[mine_h] = hb[me] + functools.reduce(
             lambda a, b: a + b, [rh[k] for k in range(1, n)]
         )
-        heat = jnp.concatenate([heat, jnp.zeros((LANES - pads_r, LANES), F32)], axis=0)
+        for d in range(1, per_row):
+            mate_copy(d).start()
+        fac = jnp.concatenate(
+            [pad_factor[...], jnp.zeros((1, half - pad_factor.shape[1]), F32)], axis=1
+        )
+        fac = jnp.concatenate([fac, fac], axis=1) * (pad_factor.shape[1] / (LIVE_DEV * n))
+        for d in range(1, per_row):
+            mate_wait(d)
+        heat = hfull[...].reshape(pads_r, LANES)
+        if pads_r < half:
+            heat = jnp.concatenate([heat, jnp.zeros((half - pads_r, LANES), F32)], axis=0)
+        heat = jnp.concatenate([heat, heat], axis=0)
         each(lambda k, to, fr: second_copy(k, to).wait_recv())
         total = s2[me] + functools.reduce(lambda a, b: a + b, [r2[k] for k in range(1, n)])
-        pad_heat = total[piece:] * pad_factor[...]
+        pad_heat = total[piece:] * fac
+        left = low[: pad_heat.shape[0]]
+        rows_l = jnp.where(left, pad_heat, 0.0)
+        if packed:
+            rows_l = jnp.concatenate([rows_l, jnp.where(left, 0.0, pad_heat)], axis=0)
         g2[me] = (
             g1[me]
             + total[:piece]
-            + jnp.dot(pad_heat, heat, precision=lax.Precision.HIGHEST, preferred_element_type=F32)
+            + jnp.dot(rows_l, heat, precision=lax.Precision.HIGHEST, preferred_element_type=F32)
         )
 
     only(me < own, reduce_second)
@@ -279,17 +336,19 @@
     each(lambda k, to, fr: only(fr < own, lambda: share_wait(6, g2, k, fr)))
     resp2 = solve(gathered(g2))
     resp_o[...] = resp2
+    out_copy(1, resp_o, resp_h).start()
     resp2 = resp2.astype(BF16)
     for i in range(chunks):
         lo, hi = i * rows_c, (i + 1) * rows_c
         defl_o[:, lo:hi] = dot_nt(resp2, basis[lo:hi, :])
 
-    each(lambda k, to, fr: ask_copy(k, to).wait_recv())
+    out_copy(2, defl_o, defl_h).start()
+
 
     def pick(k):
         out = []
         for c in range(capp // LANES):
-            idx = jnp.broadcast_to(rq[k][:, c * LANES : (c + 1) * LANES], (cases, LANES))
+            idx = jnp.broadcast_to(rq[k, 0:1, c * LANES : (c + 1) * LANES].astype(jnp.int32), (cases, LANES))
             idx_hi = lax.shift_right_logical(idx, 7)
             idx_lo = idx & (LANES - 1)
             val = jnp.zeros((cases, LANES), F32)
@@ -325,6 +384,7 @@
         return c
 
     lax.fori_loop(0, slots // LANES, place, 0)
+    out_copy(3, gap_o, gap_h).start()
 
     def drain(k, to, fr):
         def owned():
@@ -336,13 +396,35 @@
             share_copy(4, g1, k, to).wait_send()
             share_copy(6, g2, k, to).wait_send()
 
-        weight_copy(k, to).wait_send()
         ask_copy(k, to).wait_send()
         answer_copy(k, fr).wait_send()
         only(to < own, owned)
         only(me < own, mine)
 
     each(drain)
+    for d in range(1, per_row):
+        only(me < own, lambda: mate_copy(d).wait_send())
+    out_copy(0, press_o, press_h).wait()
+    out_copy(1, resp_o, resp_h).wait()
+    out_copy(2, defl_o, defl_h).wait()
+    out_copy(3, gap_o, gap_h).wait()
+
+
+def hand_over(*refs):
+    half = (len(refs) - 1) // 2
+    sems = refs[-1]
+    copies = []
+    for i in range(half):
+        src, dst = refs[i], refs[half + i]
+        for r in range(0, src.shape[0], 8):
+            part = pl.ds(r, 8)
+            copies.append(
+                pltpu.make_async_copy(src.at[part], dst.at[part], sems.at[i, r // 8])
+            )
+    for c in copies:
+        c.start()
+    for c in copies:
+        c.wait()
 
 
 def on_device(
@@ -369,24 +451,19 @@
     tiles = tile_count.shape[1]
     tile_pts = slots // tiles
     pads = pad_factor.shape[0]
-    pads_r = -(-pads // 8) * 8
-    pads_x = -(-pads // 16) * 16
     all_tiles = cases * modes // LANES
     own = min(n, all_tiles // 8)
     piece = all_tiles // own
+    per_row = cases // piece
+    rows_h = -(-pads // (8 * per_row)) * 8
+    pads_r = rows_h * per_row
+    extra = piece // 2 if piece % 16 == 0 else piece
     his = nodes // LANES
     chunks = 8
 
-    live = (
-        (jnp.arange(tile_pts, dtype=jnp.int32)[None, :] < tile_count[0][:, None])
-        .astype(F32)
-        .reshape(1, slots)
-    )
-    factor = jnp.zeros((1, LANES), F32).at[0, :pads].set(pad_factor * (pads / (LIVE_DEV * n)))
-
     vmem = pl.BlockSpec(memory_space=pltpu.VMEM)
     anyw = pl.BlockSpec(memory_space=pl.ANY)
-    return pl.pallas_call(
+    outs = pl.pallas_call(
         functools.partial(kernel, n, own),
         out_shape=(
             jax.ShapeDtypeStruct((cases, nodes), F32),
@@ -395,30 +472,35 @@
             jax.ShapeDtypeStruct((cases, nodes), F32),
         ),
         in_specs=[anyw] + [vmem] * 11 + [anyw],
-        out_specs=(vmem,) * 4,
+        out_specs=(anyw,) * 4,
         scratch_shapes=[
+            pltpu.VMEM((cases, nodes), F32),
+            pltpu.VMEM((cases, modes), F32),
+            pltpu.VMEM((cases, slots), F32),
+            pltpu.VMEM((cases, nodes), F32),
             pltpu.VMEM((nodes, modes), BF16),
             pltpu.VMEM((modes, modes), BF16),
-            pltpu.VMEM((cases + pads_x, nodes), BF16),
+            pltpu.VMEM((cases + pads_r, nodes), BF16),
             pltpu.VMEM((LANES, nodes), BF16),
-            pltpu.VMEM((n, his, LANES), F32),
-            pltpu.VMEM((n, his, LANES), F32),
+            pltpu.VMEM((1, slots), F32),
             pltpu.VMEM((his, LANES), F32),
-            pltpu.VMEM((n, 1, capp), jnp.int32),
-            pltpu.VMEM((n, 1, capp), jnp.int32),
+            pltpu.VMEM((n, 2, capp), F32),
+            pltpu.VMEM((n, 2, capp), F32),
             pltpu.VMEM((1, slots), jnp.int32),
             pltpu.VMEM((own, piece, LANES), F32),
             pltpu.VMEM((n, piece, LANES), F32),
             pltpu.VMEM((own, piece, LANES), F32),
-            pltpu.VMEM((modes // LANES, pads_r, LANES), F32),
-            pltpu.VMEM((n, pads_r, LANES), F32),
-            pltpu.VMEM((own, 2 * piece, LANES), F32),
-            pltpu.VMEM((n, 2 * piece, LANES), F32),
+            pltpu.VMEM((own, rows_h, LANES), F32),
+            pltpu.VMEM((n, rows_h, LANES), F32),
+            pltpu.VMEM((per_row, rows_h, LANES), F32),
+            pltpu.VMEM((own, piece + extra, LANES), F32),
+            pltpu.VMEM((n, piece + extra, LANES), F32),
             pltpu.VMEM((own, piece, LANES), F32),
             pltpu.VMEM((n, cases, capp), F32),
             pltpu.VMEM((n, cases, capp), F32),
-            pltpu.VMEM((cases + pads_x, modes), F32),
+            pltpu.VMEM((cases + pads_r, modes), F32),
             pltpu.SemaphoreType.DMA((chunks + 1,)),
+            pltpu.SemaphoreType.DMA((4,)),
             pltpu.SemaphoreType.DMA((8, n)),
             pltpu.SemaphoreType.DMA((8, n)),
         ],
@@ -429,17 +511,24 @@
         basis,
         thermal_load,
         pressure_load,
-        heat_coef.reshape(1, nodes),
+        heat_coef.reshape(his, LANES),
         node_pad.reshape(1, nodes),
-        factor,
+        pad_factor.reshape(1, pads),
         node_owner.reshape(1, slots),
         node_row.reshape(1, slots),
-        live,
+        tile_count,
         clearance.reshape(1, slots),
-        speed.reshape(cases, 1),
+        speed.reshape(1, cases),
         mode_scale.reshape(1, modes),
         modal_flex,
     )
+    return pl.pallas_call(
+        hand_over,
+        out_shape=tuple(jax.ShapeDtypeStruct(o.shape, o.dtype) for o in outs),
+        in_specs=[anyw] * 4,
+        out_specs=(anyw,) * 4,
+        scratch_shapes=[pltpu.SemaphoreType.DMA((4, cases // 8))],
+    )(*outs)
 
 
 def solution(mesh):

time: 87.1 us -> 106 us (1.22)
  Pallas kernels: 72.7 us -> 105 us
  local copies, waits for them, and re-layouts: 10.1 us -> 0 us
  other arithmetic: 3.27 us -> 0 us
    pallas_call x0 -> x1, Pallas kernels: none -> 44.9 us  [on_device(): pl.pallas_call(hand_over, out_shape=tuple((jax.ShapeDtypeStruct(o.shape,...]
    pallas_call x1, Pallas kernels: 72.7 us -> 60.2 us  [on_device(): pl.pallas_call(functools.partial(kernel, n, own), out_shape=(jax.ShapeDty...]
    unnamed x4 -> x0, local copies, waits for them, and re-layouts: 6.97 us -> none
    reshape x2 -> x0, local copies, waits for them, and re-layouts: 2.65 us -> none  [the longest x1 1.34 us: on_device(): speed.reshape(cases, 1)]
    another operation x2 -> x0, other arithmetic: 1.94 us -> none
    convert_element_type x1 -> x0, other arithmetic: 1.32 us -> none  [on_device(): live = (jnp.arange(tile_pts, dtype=jnp.int32)[None, :] < tile_count[0][:,...]
where the time goes in v2:
time: 106 us
  Pallas kernels  105 us (99%)
    pallas_call x1, Pallas kernels, on_device(): pl.pallas_call(functools.partial(kernel, n, own), out_shape=(jax.ShapeDty...  60.2 us
    pallas_call x1, Pallas kernels, on_device(): pl.pallas_call(hand_over, out_shape=tuple((jax.ShapeDtypeStruct(o.shape,...  44.9 us

profile of v2, /device:TPU:0, one launch (start us, length us, event | category | flops | bytes accessed | tf_op | source)
XLA Modules:
  0.0 105.8 jit_solution(17586317319745134345)
XLA Ops:
  0.6 60.2 %shard_map.156 = (f32[32,4096]{1,0:T(8,128)}, f32[32,1024]{1,0:T(8,128)}, f32[32,2048]{1,0:T(8,128)}, f32[32,4096]{1,0:T(8,128)}) custom-call(bf16[4096,1024]{1,0:T(8,128)(2,1)} %basis_h.1, bf16[32,4096]{1,0:T(8,128)(2,1)} %thermal.1, bf16[32,4096]{1,0:T(8,128)(2,1)} %pressure.1, bf16[32,128]{1,0:T(8,128)(2,1)} %bitcast.9, s32[1,4096]{1,0:T(1,128)} %bitcast.8, ...), custom_call_target="tpu_custom_call" | custom-call | tf_op jit(solution)/shard_map/pallas_call | solution.py:466
  60.8 44.9 %shard_map.157 = (f32[32,4096]{1,0:T(8,128)}, f32[32,1024]{1,0:T(8,128)}, f32[32,2048]{1,0:T(8,128)}, f32[32,4096]{1,0:T(8,128)}) custom-call(f32[32,4096]{1,0:T(8,128)} %get-tuple-element.8.refs_0_, f32[32,1024]{1,0:T(8,128)} %get-tuple-element.9.refs_1_, f32[32,2048]{1,0:T(8,128)} %get-tuple-element.10.refs_2_, f32[32,4096]{1,0:T(8,128)} %get-tuple-element.11.refs_3_), custom_call_target="tpu_custom_call" | custom-call | tf_op jit(solution)/shard_map/pallas_call | solution.py:525

commit v3 on v2

--- a/solution.py
+++ b/solution.py
@@ -367,23 +367,31 @@
 
     each(answer)
     rf[me] = pick(0)
-    each(lambda k, to, fr: remote(7, k, fs.at[k], rf.at[to], to).wait_recv())
-
-    def place(t, c):
-        part = pl.ds(pl.multiple_of(t * LANES, LANES), LANES)
-        own_t = jnp.broadcast_to(owner[:, part], (cases, LANES))
-        pos_t = jnp.broadcast_to(rank[:, part], (cases, LANES))
-        blk = own_t * (capp // LANES) + lax.shift_right_logical(pos_t, 7)
-        lane = pos_t & (LANES - 1)
-        val = jnp.zeros((cases, LANES), F32)
-        for o in range(n):
-            for s in range(capp // LANES):
-                got = jnp.take_along_axis(rf[o, :, s * LANES : (s + 1) * LANES], lane, axis=1)
-                val = jnp.where(blk == o * (capp // LANES) + s, got, val)
-        gap_o[:, part] = live[:, part] * clear[:, part] * jnp.exp(jnp.tanh(0.25 * val))
-        return c
-
-    lax.fori_loop(0, slots // LANES, place, 0)
+    blocks = capp // LANES
+
+    def place(source, last):
+        def tile(t, c):
+            part = pl.ds(pl.multiple_of(t * LANES, LANES), LANES)
+            own_t = jnp.broadcast_to(owner[:, part], (cases, LANES))
+            pos_t = jnp.broadcast_to(rank[:, part], (cases, LANES))
+            blk = (own_t - source) * blocks + lax.shift_right_logical(pos_t, 7)
+            lane = pos_t & (LANES - 1)
+            val = jnp.zeros((cases, LANES), F32) if last is None else gap_o[:, part]
+            for s in range(blocks):
+                got = jnp.take_along_axis(rf[source, :, s * LANES : (s + 1) * LANES], lane, axis=1)
+                val = jnp.where(blk == s, got, val)
+            gap_o[:, part] = val
+            return c
+
+        lax.fori_loop(0, slots // LANES, tile, 0)
+
+    def receive(k, to, fr):
+        remote(7, k, fs.at[k], rf.at[to], to).wait_recv()
+        place(to, k)
+
+    place(me, None)
+    each(receive)
+    gap_o[...] = live[...] * clear[...] * jnp.exp(jnp.tanh(0.25 * gap_o[...]))
     out_copy(3, gap_o, gap_h).start()
 
     def drain(k, to, fr):
@@ -411,20 +419,19 @@
 
 
 def hand_over(*refs):
-    half = (len(refs) - 1) // 2
+    count = (len(refs) - 1) // 3
     sems = refs[-1]
-    copies = []
-    for i in range(half):
-        src, dst = refs[i], refs[half + i]
-        for r in range(0, src.shape[0], 8):
-            part = pl.ds(r, 8)
-            copies.append(
-                pltpu.make_async_copy(src.at[part], dst.at[part], sems.at[i, r // 8])
-            )
-    for c in copies:
+    ins, outs, held = (refs[i * count : (i + 1) * count] for i in range(3))
+    order = (3, 1, 0, 2)
+    first = [pltpu.make_async_copy(ins[i], held[i], sems.at[0, i]) for i in order]
+    second = [pltpu.make_async_copy(held[i], outs[i], sems.at[1, i]) for i in order]
+    for c in first:
         c.start()
-    for c in copies:
+    for c, d in zip(first, second):
         c.wait()
+        d.start()
+    for d in second:
+        d.wait()
 
 
 def on_device(
@@ -527,7 +534,8 @@
         out_shape=tuple(jax.ShapeDtypeStruct(o.shape, o.dtype) for o in outs),
         in_specs=[anyw] * 4,
         out_specs=(anyw,) * 4,
-        scratch_shapes=[pltpu.SemaphoreType.DMA((4, cases // 8))],
+        scratch_shapes=[pltpu.VMEM(o.shape, o.dtype) for o in outs] + [pltpu.SemaphoreType.DMA((2, 4))],
+        compiler_params=pltpu.CompilerParams(vmem_limit_bytes=8 * 1024 * 1024),
     )(*outs)
 
 

time: 106 us -> 79.5 us (0.75)
  Pallas kernels: 105 us -> 74.7 us
  local copies, waits for them, and re-layouts: 0 us -> 3.93 us
    pallas_call x1, Pallas kernels: 44.9 us -> 1.41 us  [on_device(): pl.pallas_call(hand_over, out_shape=tuple((jax.ShapeDtypeStruct(o.shape,...]
    pallas_call x1, Pallas kernels: 60.2 us -> 73.3 us  [on_device(): pl.pallas_call(functools.partial(kernel, n, own), out_shape=(jax.ShapeDty...]
    unnamed x0 -> x8, local copies, waits for them, and re-layouts: none -> 3.93 us
where the time goes in v3:
time: 79.5 us; the launch traced here: 79.3 us
  Pallas kernels  74.7 us (94%)
  local copies, waits for them, and re-layouts  3.93 us (5%)
    pallas_call x1, Pallas kernels, on_device(): pl.pallas_call(functools.partial(kernel, n, own), out_shape=(jax.ShapeDty...  73.3 us
    unnamed x8, local copies, waits for them, and re-layouts  3.93 us

profile of v3, /device:TPU:0, one launch (start us, length us, event | category | flops | bytes accessed | tf_op | source)
XLA Modules:
  0.0 79.3 jit_solution(11320437060962785528)
XLA Ops:
  0.6 73.3 %shard_map.156 = (f32[32,4096]{1,0:T(8,128)}, f32[32,1024]{1,0:T(8,128)}, f32[32,2048]{1,0:T(8,128)}, f32[32,4096]{1,0:T(8,128)}) custom-call(bf16[4096,1024]{1,0:T(8,128)(2,1)} %basis_h.1, bf16[32,4096]{1,0:T(8,128)(2,1)} %thermal.1, bf16[32,4096]{1,0:T(8,128)(2,1)} %pressure.1, bf16[32,128]{1,0:T(8,128)(2,1)} %bitcast.9, s32[1,4096]{1,0:T(1,128)} %bitcast.8, ...), custom_call_target="tpu_custom_call" | custom-call | tf_op jit(solution)/shard_map/pallas_call | solution.py:473
  73.9 0.0 copy-start
  73.9 1.0 %copy-done = f32[32,4096]{1,0:T(8,128)S(1)} copy-done((f32[32,4096]{1,0:T(8,128)S(1)}, f32[32,4096]{1,0:T(8,128)}, u32[]{:S(2)}) %copy-start) | copy-done | bytes 524312
  74.9 0.0 copy-start.1
  74.9 1.0 %copy-done.1 = f32[32,4096]{1,0:T(8,128)S(1)} copy-done((f32[32,4096]{1,0:T(8,128)S(1)}, f32[32,4096]{1,0:T(8,128)}, u32[]{:S(2)}) %copy-start.1) | copy-done | bytes 524312
  76.0 0.0 copy-start.2
  76.0 0.9 %copy-done.2 = f32[32,2048]{1,0:T(8,128)S(1)} copy-done((f32[32,2048]{1,0:T(8,128)S(1)}, f32[32,2048]{1,0:T(8,128)}, u32[]{:S(2)}) %copy-start.2) | copy-done | bytes 262168
  76.9 0.0 copy-start.3
  76.9 0.9 %copy-done.3 = f32[32,1024]{1,0:T(8,128)S(1)} copy-done((f32[32,1024]{1,0:T(8,128)S(1)}, f32[32,1024]{1,0:T(8,128)}, u32[]{:S(2)}) %copy-start.3) | copy-done | bytes 131096
  77.8 1.4 %shard_map.157 = (f32[32,4096]{1,0:T(8,128)}, f32[32,1024]{1,0:T(8,128)}, f32[32,2048]{1,0:T(8,128)}, f32[32,4096]{1,0:T(8,128)}) custom-call(f32[32,4096]{1,0:T(8,128)S(1)} %copy-done, f32[32,1024]{1,0:T(8,128)S(1)} %copy-done.3, f32[32,2048]{1,0:T(8,128)S(1)} %copy-done.2, f32[32,4096]{1,0:T(8,128)S(1)} %copy-done.1), custom_call_target="tpu_custom_call" | custom-call | tf_op jit(solution)/shard_map/pallas_call | solution.py:532
Async XLA Ops:
  73.9 1.0 %copy-start = (f32[32,4096]{1,0:T(8,128)S(1)}, f32[32,4096]{1,0:T(8,128)}, u32[]{:S(2)}) copy-start(f32[32,4096]{1,0:T(8,128)} %get-tuple-element.8.refs_0_) | copy-start | bytes 1572868
  74.9 1.0 %copy-start.1 = (f32[32,4096]{1,0:T(8,128)S(1)}, f32[32,4096]{1,0:T(8,128)}, u32[]{:S(2)}) copy-start(f32[32,4096]{1,0:T(8,128)} %get-tuple-element.11.refs_3_) | copy-start | bytes 1572868
  76.0 0.9 %copy-start.2 = (f32[32,2048]{1,0:T(8,128)S(1)}, f32[32,2048]{1,0:T(8,128)}, u32[]{:S(2)}) copy-start(f32[32,2048]{1,0:T(8,128)} %get-tuple-element.10.refs_2_) | copy-start | bytes 786436
  76.9 0.9 %copy-start.3 = (f32[32,1024]{1,0:T(8,128)S(1)}, f32[32,1024]{1,0:T(8,128)}, u32[]{:S(2)}) copy-start(f32[32,1024]{1,0:T(8,128)} %get-tuple-element.9.refs_1_) | copy-start | bytes 393220

commit v4 on v2

--- a/solution.py
+++ b/solution.py
@@ -411,20 +411,19 @@
 
 
 def hand_over(*refs):
-    half = (len(refs) - 1) // 2
+    count = (len(refs) - 1) // 3
     sems = refs[-1]
-    copies = []
-    for i in range(half):
-        src, dst = refs[i], refs[half + i]
-        for r in range(0, src.shape[0], 8):
-            part = pl.ds(r, 8)
-            copies.append(
-                pltpu.make_async_copy(src.at[part], dst.at[part], sems.at[i, r // 8])
-            )
-    for c in copies:
+    ins, outs, held = (refs[i * count : (i + 1) * count] for i in range(3))
+    order = (3, 1, 0, 2)
+    first = [pltpu.make_async_copy(ins[i], held[i], sems.at[0, i]) for i in order]
+    second = [pltpu.make_async_copy(held[i], outs[i], sems.at[1, i]) for i in order]
+    for c in first:
         c.start()
-    for c in copies:
+    for c, d in zip(first, second):
         c.wait()
+        d.start()
+    for d in second:
+        d.wait()
 
 
 def on_device(
@@ -527,7 +526,8 @@
         out_shape=tuple(jax.ShapeDtypeStruct(o.shape, o.dtype) for o in outs),
         in_specs=[anyw] * 4,
         out_specs=(anyw,) * 4,
-        scratch_shapes=[pltpu.SemaphoreType.DMA((4, cases // 8))],
+        scratch_shapes=[pltpu.VMEM(o.shape, o.dtype) for o in outs] + [pltpu.SemaphoreType.DMA((2, 4))],
+        compiler_params=pltpu.CompilerParams(vmem_limit_bytes=60 * 1024 * 1024),
     )(*outs)
 
 

time: 106 us -> 63.2 us (0.60)
  Pallas kernels: 105 us -> 62.4 us
    pallas_call x1, Pallas kernels: 44.9 us -> 2.2 us  [on_device(): pl.pallas_call(hand_over, out_shape=tuple((jax.ShapeDtypeStruct(o.shape,...]
where the time goes in v4:
time: 63.2 us; the launch traced here: 63 us
  Pallas kernels  62.4 us (99%)
  between operations  0.64 us (1%)
    pallas_call x1, Pallas kernels, on_device(): pl.pallas_call(functools.partial(kernel, n, own), out_shape=(jax.ShapeDty...  60.2 us
    pallas_call x1, Pallas kernels, on_device(): pl.pallas_call(hand_over, out_shape=tuple((jax.ShapeDtypeStruct(o.shape,...  2.2 us

profile of v4, /device:TPU:0, one launch (start us, length us, event | category | flops | bytes accessed | tf_op | source)
XLA Modules:
  0.0 63.0 jit_solution(15872739687663166026)
XLA Ops:
  0.6 60.2 %shard_map.156 = (f32[32,4096]{1,0:T(8,128)}, f32[32,1024]{1,0:T(8,128)}, f32[32,2048]{1,0:T(8,128)}, f32[32,4096]{1,0:T(8,128)}) custom-call(bf16[4096,1024]{1,0:T(8,128)(2,1)} %basis_h.1, bf16[32,4096]{1,0:T(8,128)(2,1)} %thermal.1, bf16[32,4096]{1,0:T(8,128)(2,1)} %pressure.1, bf16[32,128]{1,0:T(8,128)(2,1)} %bitcast.9, s32[1,4096]{1,0:T(1,128)} %bitcast.8, ...), custom_call_target="tpu_custom_call" | custom-call | tf_op jit(solution)/shard_map/pallas_call | solution.py:465
  60.8 2.2 %shard_map.157 = (f32[32,4096]{1,0:T(8,128)}, f32[32,1024]{1,0:T(8,128)}, f32[32,2048]{1,0:T(8,128)}, f32[32,4096]{1,0:T(8,128)}) custom-call(f32[32,4096]{1,0:T(8,128)} %get-tuple-element.8.refs_0_, f32[32,1024]{1,0:T(8,128)} %get-tuple-element.9.refs_1_, f32[32,2048]{1,0:T(8,128)} %get-tuple-element.10.refs_2_, f32[32,4096]{1,0:T(8,128)} %get-tuple-element.11.refs_3_), custom_call_target="tpu_custom_call" | custom-call | tf_op jit(solution)/shard_map/pallas_call | solution.py:524

commit v5 on v4

--- a/solution.py
+++ b/solution.py
@@ -212,7 +212,6 @@
         remote(phase, k, g.at[fr], g.at[fr], fr).wait_recv()
 
     only(me < own, lambda: each(lambda k, to, fr: share_copy(4, g1, k, to).start()))
-    each(lambda k, to, fr: only(to < own, lambda: heat_copy(k, to).start()))
     each(lambda k, to, fr: ask_copy(k, to).wait_recv())
     both = jnp.zeros((his, 2 * LANES), F32)
     for k in range(n):
@@ -231,6 +230,7 @@
     )
     speed_c = jnp.sum(jnp.where(eye, speed[...], 0.0), axis=1, keepdims=True)
     each(lambda k, to, fr: only(fr < own, lambda: share_wait(4, g1, k, fr)))
+    each(lambda k, to, fr: only(to < own, lambda: heat_copy(k, to).start()))
 
     def gathered(g):
         flat = g[...].reshape(own * piece, LANES)

time: 63.2 us -> 61.9 us (0.979)
  Pallas kernels: 62.4 us -> 61.1 us
    pallas_call x1, Pallas kernels: 60.2 us -> 58.9 us  [on_device(): pl.pallas_call(functools.partial(kernel, n, own), out_shape=(jax.ShapeDty...]
where the time goes in v5:
time: 61.9 us; the launch traced here: 61.8 us
  Pallas kernels  61.1 us (99%)
  between operations  0.64 us (1%)
    pallas_call x1, Pallas kernels, on_device(): pl.pallas_call(functools.partial(kernel, n, own), out_shape=(jax.ShapeDty...  58.9 us
    pallas_call x1, Pallas kernels, on_device(): pl.pallas_call(hand_over, out_shape=tuple((jax.ShapeDtypeStruct(o.shape,...  2.2 us

profile of v5, /device:TPU:0, one launch (start us, length us, event | category | flops | bytes accessed | tf_op | source)
XLA Modules:
  0.0 61.8 jit_solution(17122047466909837210)
XLA Ops:
  0.6 58.9 %shard_map.156 = (f32[32,4096]{1,0:T(8,128)}, f32[32,1024]{1,0:T(8,128)}, f32[32,2048]{1,0:T(8,128)}, f32[32,4096]{1,0:T(8,128)}) custom-call(bf16[4096,1024]{1,0:T(8,128)(2,1)} %basis_h.1, bf16[32,4096]{1,0:T(8,128)(2,1)} %thermal.1, bf16[32,4096]{1,0:T(8,128)(2,1)} %pressure.1, bf16[32,128]{1,0:T(8,128)(2,1)} %bitcast.9, s32[1,4096]{1,0:T(1,128)} %bitcast.8, ...), custom_call_target="tpu_custom_call" | custom-call | tf_op jit(solution)/shard_map/pallas_call | solution.py:465
  59.5 2.2 %shard_map.157 = (f32[32,4096]{1,0:T(8,128)}, f32[32,1024]{1,0:T(8,128)}, f32[32,2048]{1,0:T(8,128)}, f32[32,4096]{1,0:T(8,128)}) custom-call(f32[32,4096]{1,0:T(8,128)} %get-tuple-element.8.refs_0_, f32[32,1024]{1,0:T(8,128)} %get-tuple-element.9.refs_1_, f32[32,2048]{1,0:T(8,128)} %get-tuple-element.10.refs_2_, f32[32,4096]{1,0:T(8,128)} %get-tuple-element.11.refs_3_), custom_call_target="tpu_custom_call" | custom-call | tf_op jit(solution)/shard_map/pallas_call | solution.py:524
